TPU v7x, 128 devices: a whole 4x4x4 slice. The times are simulated.
128 devices in a mesh: row: 2 (over core), col: 4 (over x), rep: 16 (over z, y).
Axes of the slice: x: 4, y: 4, z: 4, core: 2. Of those that a mesh axis runs over, the one named last changes fastest.
Arguments:
- hamiltonian: bfloat16 [7168, 7168], P('row', 'col'), may hold values from -1 to 1, as said below
- pattern: int32 [56, 56], P('row', 'col'), may hold values from 0 to 1, as said below
Outputs:
- sign_matrix: bfloat16 [7168, 7168], P('row', 'col')
Inputs may be any that keep to these rules, and one draw needn't show every extreme that they name: `hamiltonian`: a symmetric matrix. `pattern`: symmetric; ones on the block diagonal and on the blocks next to it, cyclically.
All inputs are finite; a program needn't handle non-finite values.
Results may differ from a plain program's by a relative error of at most 0.015.
Values may be sent and summed in bfloat16 or wider, within the bound.
No kernel may reach another device: no remote copies, remote signals or barrier semaphores. Data moves between devices by JAX's collectives and lax.ppermute only.
A program may use at most 256 MiB of HBM per device.

v0:
```python
import jax
import jax.numpy as jnp
from jax import lax
from jax.sharding import PartitionSpec as P


def expand(pattern, block_size):
    retained = pattern.astype(jnp.float32)
    block_rows, block_cols = pattern.shape
    grown = jnp.broadcast_to(
        retained[:, None, :, None], (block_rows, block_size, block_cols, block_size)
    )
    return grown.reshape(block_rows * block_size, block_cols * block_size)


def column_slab(matrix, replica, replicas, slab_rows):
    height, tile_width = matrix.shape
    shaped = matrix.reshape(height, tile_width // (replicas * slab_rows), replicas, slab_rows)
    selected = lax.dynamic_slice_in_dim(shaped, replica, 1, 2)
    return selected.reshape(height, tile_width // replicas)


def row_slab(matrix, replica, replicas, slab_rows):
    height, tile_width = matrix.shape
    shaped = matrix.reshape(height // (replicas * slab_rows), replicas, slab_rows, tile_width)
    selected = lax.dynamic_slice_in_dim(shaped, replica, 1, 1)
    return selected.reshape(height // replicas, tile_width)


def contract(panel_cols, right_rows):
    return jnp.dot(
        panel_cols,
        lax.all_gather(right_rows, "row", axis=0, tiled=True),
        preferred_element_type=jnp.float32,
    )


def shards(hamiltonian, pattern):
    height, tile_width = hamiltonian.shape
    replicas = lax.axis_size("rep")
    slab_rows = height // (lax.axis_size("col") * replicas)
    replica = lax.axis_index("rep")
    retained = expand(pattern, height // pattern.shape[0])
    current = (hamiltonian.astype(jnp.float32) * retained).astype(jnp.bfloat16)
    panel_cols = lax.all_gather(
        column_slab(current, replica, replicas, slab_rows), "col", axis=1, tiled=True
    )
    square_part = contract(panel_cols, row_slab(current, replica, replicas, slab_rows))
    summed = lax.psum(square_part.astype(jnp.bfloat16), "rep").astype(jnp.float32)
    square = (summed * retained).astype(jnp.bfloat16)
    square_rows = row_slab(square, replica, replicas, slab_rows)
    cubed_part = contract(panel_cols, square_rows)
    cubed = lax.psum(cubed_part.astype(jnp.bfloat16), "rep").astype(jnp.float32)
    current = ((1.5 * current.astype(jnp.float32) - 0.5 * cubed) * retained).astype(jnp.bfloat16)
    return current


def solution(mesh):
    in_specs = (P("row", "col"), P("row", "col"))
    out_specs = P("row", "col")
    return jax.shard_map(shards, mesh=mesh, in_specs=in_specs, out_specs=out_specs, check_vma=False)
```

profile of v0, /device:TPU:1, one launch (start us, length us, event | category | flops | bytes accessed | tf_op | source)
XLA Modules:
  0.0 559.2 jit_solution(17307685097631225118)
XLA Ops:
  6.5 0.7 convert_element_type.31
  7.2 0.1 copy.4
  7.3 11.6 %broadcast_in_dim.2 = f32[28,128,14,128]{3,2,1,0:T(8,128)} broadcast(f32[28,14]{1,0:T(8,128)S(1)} %copy.4), dimensions={0,2} | broadcast | bytes 25691680 | tf_op jit(solution)/shard_map/broadcast_in_dim | solution.py:10
  19.0 18.7 %fusion = bf16[3584,1792]{1,0:T(8,128)(2,1)S(1)} fusion(bf16[3584,1792]{1,0:T(8,128)(2,1)} %param.2, f32[448,8,14,128]{3,2,1,0:T(8,128)} %bitcast.24), kind=kLoop, calls=%fused_computation.3 | loop fusion | flops 19267584 | bytes 51380224 | tf_op jit(solution)/shard_map/convert_element_type | solution.py:44
  37.7 4.9 copy-done
  42.6 1.0 constant_dynamic-slice_fusion.1
  43.6 0.0 all-gather.4.cloned.1.call-start
  43.6 18.2 %copy.5 = bf16[3584,1792]{0,1:T(8,128)(2,1)} copy(bf16[3584,1792]{1,0:T(8,128)(2,1)} %copy-done) | data formatting | bytes 25690112 | tf_op jit(solution)/shard_map/convert_element_type | solution.py:44
  61.9 2.1 constant_dynamic-slice_fusion.2
  64.0 0.0 all-gather.4.cloned.1.call-update
  64.0 0.0 all-reduce.3.cloned.1.call-start
  64.0 0.0 all-gather.6.cloned.1.call-done
  64.1 43.3 %all-gather.4.cloned.1.call-done = bf16[3584,448]{0,1:T(8,128)(2,1)} async-done(((bf16[3584,112]{0,1:T(8,128)(2,1)}), bf16[3584,448]{0,1:T(8,128)(2,1)}) %all-gather.4.cloned.1.call-update) | async-done | bytes 3211280 | tf_op jit(solution)/shard_map/all_gather | solution.py:45
  107.3 11.8 %convolution_convert_fusion.1 = bf16[3584,1792]{1,0:T(8,128)(2,1)} fusion(bf16[3584,448]{0,1:T(8,128)(2,1)} %all-gather.4.cloned.1.call-done, bf16[448,1792]{1,0:T(8,128)(2,1)} %all-gather.6.cloned.1.call-done), kind=kOutput, calls=%fused_computation.7 | convolution fusion | flops 5761007616 | bytes 17661952 | tf_op jit(solution)/shard_map/dot_general | solution.py:31
  119.1 0.0 all-reduce.3.cloned.1.call-update
  119.1 0.0 all-gather.8.cloned.1.call-start
  119.2 181.5 %all-reduce.3.cloned.1.call-done = bf16[3584,1792]{1,0:T(8,128)(2,1)} async-done(((bf16[3584,1792]{1,0:T(8,128)(2,1)}), bf16[3584,1792]{1,0:T(8,128)(2,1)}) %all-reduce.3.cloned.1.call-update) | async-done | bytes 12845072 | tf_op jit(solution)/shard_map/psum | solution.py:49
  300.7 18.7 %fusion.1 = bf16[3584,1792]{1,0:T(8,128)(2,1)S(1)} fusion(bf16[3584,1792]{1,0:T(8,128)(2,1)} %all-reduce.3.cloned.1.call-done, f32[448,8,14,128]{3,2,1,0:T(8,128)} %bitcast.25), kind=kLoop, calls=%fused_computation.4 | loop fusion | flops 19267584 | bytes 51380224 | tf_op jit(solution)/shard_map/convert_element_type | solution.py:50
  319.5 0.9 constant_dynamic-slice_fusion
  320.4 0.2 all-reduce.5.cloned.1.call-start
  320.7 12.6 %all-gather.8.cloned.1.call-done = bf16[448,1792]{1,0:T(8,128)(2,1)} async-done(((bf16[224,1792]{1,0:T(8,128)(2,1)}), bf16[448,1792]{1,0:T(8,128)(2,1)}) %all-gather.8.cloned.1.call-update) | async-done | bytes 1605648 | tf_op jit(solution)/shard_map/all_gather | solution.py:33
  333.2 11.3 %convolution_convert_fusion = bf16[3584,1792]{1,0:T(8,128)(2,1)} fusion(bf16[3584,448]{0,1:T(8,128)(2,1)S(1)} %copy-done.1, bf16[448,1792]{1,0:T(8,128)(2,1)} %all-gather.8.cloned.1.call-done), kind=kOutput, calls=%fused_computation.6 | convolution fusion | flops 5761007616 | bytes 17661952 | tf_op jit(solution)/shard_map/dot_general | solution.py:31
  344.5 182.3 %all-reduce.5.cloned.1.call-done = bf16[3584,1792]{1,0:T(8,128)(2,1)} async-done(((bf16[3584,1792]{1,0:T(8,128)(2,1)}), bf16[3584,1792]{1,0:T(8,128)(2,1)}) %all-reduce.5.cloned.1.call-update) | async-done | bytes 12845072 | tf_op jit(solution)/shard_map/psum | solution.py:53
  526.9 25.8 %fusion.2 = bf16[3584,1792]{1,0:T(8,128)(2,1)} fusion(bf16[3584,1792]{1,0:T(8,128)(2,1)} %all-reduce.5.cloned.1.call-done, f32[448,8,14,128]{3,2,1,0:T(8,128)} %bitcast.26, bf16[3584,1792]{1,0:T(8,128)(2,1)} %param.2), kind=kLoop, calls=%fused_computation.5 | loop fusion | flops 64225280 | bytes 64225280 | tf_op jit(solution)/shard_map/convert_element_type | solution.py:54
  (7 shorter events, 0.1 us)
Async XLA Ops:
  6.5 57.5 %all-gather.6.cloned.1.call-start = ((), (), s32[]{:S(2)}) async-start(), calls=%async_computation.1 | async-start | bytes 2408448 | tf_op jit(solution)/shard_map/all_gather | solution.py:33
  37.7 4.9 copy-start
  43.6 63.7 %all-gather.4.cloned.1.call-start = ((), (), s32[]{:S(2)}) async-start(), calls=%async_computation | async-start | bytes 4014080 | tf_op jit(solution)/shard_map/all_gather | solution.py:45
  64.0 236.7 %all-reduce.3.cloned.1.call-start = ((), (), s32[]{:S(2)}) async-start(), calls=%async_computation.2 | async-start | bytes 25690112 | tf_op jit(solution)/shard_map/psum | solution.py:49
  119.1 214.1 %copy-start.1 = (bf16[3584,448]{0,1:T(8,128)(2,1)S(1)}, bf16[3584,448]{0,1:T(8,128)(2,1)}, u32[]{:S(2)}) copy-start(bf16[3584,448]{0,1:T(8,128)(2,1)} %all-gather.4.cloned.1.call-done) | copy-start | bytes 9633796
  119.1 214.1 %all-gather.8.cloned.1.call-start = ((), (), s32[]{:S(2)}) async-start(), calls=%async_computation.3 | async-start | bytes 2408448 | tf_op jit(solution)/shard_map/all_gather | solution.py:33
  320.4 206.4 %all-reduce.5.cloned.1.call-start = ((), (), s32[]{:S(2)}) async-start(), calls=%async_computation.4 | async-start | bytes 25690112 | tf_op jit(solution)/shard_map/psum | solution.py:53
Sparse Core Ops, SparseCore 0:
  43.7 16.1 all-gather.5
  64.1 43.1 all-gather.3
  119.2 181.4 all-reduce.2
  320.5 12.6 all-gather.7
  344.7 182.1 all-reduce.4
where the time goes:
time: 560 us; the launch traced here: 559 us
  waiting for transfers between devices  420 us (75%)
  other arithmetic  64 us (11%)
  local copies, waits for them, and re-layouts  38.8 us (7%)
  matrix products  23 us (4%)
  between operations  13.2 us (2%)
    psum x1, waiting for transfers between devices, shards(): cubed = lax.psum(cubed_part.astype(jnp.bfloat16), 'rep').astype(jnp.float32)  182 us
    psum x1, waiting for transfers between devices, shards(): lax.psum(square_part.astype(jnp.bfloat16), 'rep').astype(jnp.float32)  182 us
    all_gather x1, waiting for transfers between devices, shards(): lax.all_gather(column_slab(current, replica, replicas, slab_rows), 'col',...  43.3 us
    convert_element_type x1, other arithmetic, shards(): ((1.5 * current.astype(jnp.float32) - 0.5 * cubed) * retained).astype(jnp...  25.8 us
    dot_general x2, matrix products, contract(): jnp.dot(panel_cols, lax.all_gather(right_rows, 'row', axis=0, tiled=True)...  23 us
    convert_element_type x1, other arithmetic, shards(): current = (hamiltonian.astype(jnp.float32) * retained).astype(jnp.bfloat16)  18.7 us
    convert_element_type x1, other arithmetic, shards(): square = (summed * retained).astype(jnp.bfloat16)  18.7 us
    convert_element_type x1, local copies, waits for them, and re-layouts, shards(): current = (hamiltonian.astype(jnp.float32) * retained).astype(jnp.bfloat16)  18.2 us
  transfers between devices with their start and end apart: 5, of which 4 were waited for; matrix products, arithmetic and copies ran while one was open for 4% of the time, Pallas kernels for 0%

commit v1 on v0

v1 whole, which is shorter than its diff:
```python
import functools

import jax
import jax.numpy as jnp
from jax import lax
from jax.experimental import pallas as pl
from jax.experimental.pallas import tpu as pltpu
from jax.sharding import PartitionSpec as P

BS = 128
UNIT = 16
TIERS = (176, 192, 208, 224, 256, 320, 400)
VMEM_LIMIT = 60 * 1024 * 1024


def params():
    return pltpu.CompilerParams(vmem_limit_bytes=VMEM_LIMIT)


def mask_kernel(pat_ref, rep_ref, h_ref, x_ref, g_ref, pick_ref, *, reps):
    step = pl.program_id(0)
    stripe, width = h_ref.shape
    units = pick_ref.shape[0]

    @pl.when(step == 0)
    def _():
        u = lax.broadcasted_iota(jnp.int32, (units, width), 0)
        c = lax.broadcasted_iota(jnp.int32, (units, width), 1)
        target = (u // UNIT) * (reps * UNIT) + rep_ref[0] * UNIT + u % UNIT
        pick_ref[...] = jnp.where(c == target, 1.0, 0.0).astype(jnp.bfloat16)

    for a in range(stripe // BS):
        for b in range(width // BS):
            kept = pat_ref[step * (stripe // BS) + a, b].astype(jnp.float32)
            rows, cols = pl.ds(a * BS, BS), pl.ds(b * BS, BS)
            x_ref[rows, cols] = (h_ref[rows, cols].astype(jnp.float32) * kept).astype(jnp.bfloat16)
    g_ref[...] = lax.dot_general(
        pick_ref[...], x_ref[...], (((1,), (1,)), ((), ())), preferred_element_type=jnp.float32
    ).astype(jnp.bfloat16)


def mask_and_pick(tile, pattern, rep, reps, stripe=512):
    height, width = tile.shape
    units = width // reps
    return pl.pallas_call(
        functools.partial(mask_kernel, reps=reps),
        grid=(height // stripe,),
        in_specs=[
            pl.BlockSpec(memory_space=pltpu.SMEM),
            pl.BlockSpec(memory_space=pltpu.SMEM),
            pl.BlockSpec((stripe, width), lambda i: (i, 0)),
        ],
        out_specs=[
            pl.BlockSpec((stripe, width), lambda i: (i, 0)),
            pl.BlockSpec((units, stripe), lambda i: (0, i)),
        ],
        out_shape=[
            jax.ShapeDtypeStruct((height, width), jnp.bfloat16),
            jax.ShapeDtypeStruct((units, height), jnp.bfloat16),
        ],
        scratch_shapes=[pltpu.VMEM((units, width), jnp.bfloat16)],
        compiler_params=params(),
        name="mask_and_pick",
    )(pattern, rep, tile)


def cube_kernel(pat_ref, g_ref, q_ref, out_ref, part_ref, count_ref, *, slots):
    step = pl.program_id(0)
    stripe = g_ref.shape[1]
    width = q_ref.shape[1]

    @pl.when(step == 0)
    def _():
        count_ref[0] = 0

    turned = g_ref[...].T
    for c in range(width // (2 * BS)):
        acc = jnp.dot(
            turned, q_ref[:, 2 * BS * c : 2 * BS * (c + 1)], preferred_element_type=jnp.float32
        ).astype(jnp.bfloat16)
        part_ref[2 * c] = acc[:, :BS]
        part_ref[2 * c + 1] = acc[:, BS:]
    count = count_ref[0]
    for a in range(stripe // BS):
        for b in range(width // BS):
            kept = pat_ref[step * (stripe // BS) + a, b]
            slot = jnp.minimum(count, slots - 1)

            @pl.when(kept != 0)
            def _():
                out_ref[slot] = part_ref[b, a * BS : (a + 1) * BS, :]

            count = count + kept
    count_ref[0] = count

    @pl.when(step == pl.num_programs(0) - 1)
    def _():
        def clear(s, carry):
            out_ref[s] = jnp.zeros((BS, BS), jnp.bfloat16)
            return carry

        lax.fori_loop(jnp.minimum(count, slots), slots, clear, 0)


def cube_part(pattern, rows, square_rows, slots, stripe=512):
    depth, height = rows.shape
    width = square_rows.shape[1]
    return pl.pallas_call(
        functools.partial(cube_kernel, slots=slots),
        grid=(height // stripe,),
        in_specs=[
            pl.BlockSpec(memory_space=pltpu.SMEM),
            pl.BlockSpec((depth, stripe), lambda i: (0, i)),
            pl.BlockSpec((depth, width), lambda i: (0, 0)),
        ],
        out_specs=pl.BlockSpec((slots, BS, BS), lambda i: (0, 0, 0)),
        out_shape=jax.ShapeDtypeStruct((slots, BS, BS), jnp.bfloat16),
        scratch_shapes=[
            pltpu.VMEM((width // BS, stripe, BS), jnp.bfloat16),
            pltpu.SMEM((1,), jnp.int32),
        ],
        compiler_params=params(),
        name="cube_part",
    )(pattern, rows, square_rows)


def finish_kernel(pat_ref, h_ref, cubed_ref, out_ref, count_ref, *, slots):
    step = pl.program_id(0)
    stripe, width = h_ref.shape

    @pl.when(step == 0)
    def _():
        count_ref[0] = 0

    count = count_ref[0]
    for a in range(stripe // BS):
        for b in range(width // BS):
            kept = pat_ref[step * (stripe // BS) + a, b]
            slot = jnp.minimum(count, slots - 1)
            rows, cols = pl.ds(a * BS, BS), pl.ds(b * BS, BS)
            value = 1.5 * h_ref[rows, cols].astype(jnp.float32) - 0.5 * cubed_ref[slot].astype(
                jnp.float32
            )
            out_ref[rows, cols] = jnp.where(kept != 0, value, 0.0).astype(jnp.bfloat16)
            count = count + kept
    count_ref[0] = count


def finish(pattern, tile, cubed, slots, stripe=512):
    height, width = tile.shape
    return pl.pallas_call(
        functools.partial(finish_kernel, slots=slots),
        grid=(height // stripe,),
        in_specs=[
            pl.BlockSpec(memory_space=pltpu.SMEM),
            pl.BlockSpec((stripe, width), lambda i: (i, 0)),
            pl.BlockSpec((slots, BS, BS), lambda i: (0, 0, 0)),
        ],
        out_specs=pl.BlockSpec((stripe, width), lambda i: (i, 0)),
        out_shape=jax.ShapeDtypeStruct((height, width), jnp.bfloat16),
        scratch_shapes=[pltpu.SMEM((1,), jnp.int32)],
        compiler_params=params(),
        name="finish",
    )(pattern, tile, cubed)


def gather_rows(piece):
    cols = lax.axis_size("col")
    up = [(i, (i + 1) % cols) for i in range(cols)]
    down = [(i, (i - 1) % cols) for i in range(cols)]
    before = lax.ppermute(piece, "col", up)
    after = lax.ppermute(piece, "col", down)
    cut = 64
    far_top = lax.ppermute(before[:cut], "col", up)
    far_bottom = lax.ppermute(after[cut:], "col", down)
    return jnp.concatenate([piece, before, after, far_top, far_bottom], axis=0)


def shards(hamiltonian, pattern):
    height, width = hamiltonian.shape
    reps = lax.axis_size("rep")
    cols = lax.axis_size("col")
    rep = lax.axis_index("rep")
    col = lax.axis_index("col")
    block_rows, block_cols = pattern.shape

    patterns = lax.all_gather(pattern, ("row", "col"), axis=0).reshape(-1, cols, block_rows, block_cols)
    most = jnp.max(jnp.sum(patterns, axis=(2, 3)))
    tier = sum((most > t).astype(jnp.int32) for t in TIERS[:-1])
    panel = lax.dynamic_index_in_dim(patterns, col, 1, keepdims=False).reshape(-1, block_cols)

    current, piece = mask_and_pick(hamiltonian, pattern, rep.reshape(1), reps)
    rows = gather_rows(piece)

    unit = jnp.arange(width // (reps * UNIT))
    owners = (col + jnp.array([0, cols - 1, 1, 2])) % cols
    unit_block = (owners[:, None] * width + unit[None, :] * (reps * UNIT) + rep * UNIT) // BS
    kept = panel[unit_block.reshape(-1)].astype(jnp.bfloat16)
    mask = jnp.broadcast_to(kept[:, None, :, None], (kept.shape[0], UNIT, block_cols, BS))
    mask = mask.reshape(rows.shape[0], width)

    part = jnp.dot(rows, current, preferred_element_type=jnp.float32)
    other = lax.ppermute(part.astype(jnp.bfloat16), "row", [(0, 1), (1, 0)])
    square_rows = jnp.where(mask != 0, part + other.astype(jnp.float32), 0.0).astype(jnp.bfloat16)

    def branch(slots):
        def run(pattern, rows, square_rows, hamiltonian):
            packed = cube_part(pattern, rows, square_rows, slots)
            cubed = lax.psum(packed, "rep")
            return finish(pattern, hamiltonian, cubed, slots)

        return run

    return lax.switch(tier, [branch(t) for t in TIERS], pattern, rows, square_rows, hamiltonian)


def solution(mesh):
    in_specs = (P("row", "col"), P("row", "col"))
    out_specs = P("row", "col")
    return jax.shard_map(shards, mesh=mesh, in_specs=in_specs, out_specs=out_specs, check_vma=False)
```

time: 560 us -> 277 us (0.49)
  waiting for transfers between devices: 420 us -> 160 us
  other arithmetic: 64 us -> 5.27 us
  Pallas kernels: 0 us -> 47.1 us
  local copies, waits for them, and re-layouts: 38.8 us -> 4.72 us
  blocking collectives: 0 us -> 21.4 us
  matrix products: 23 us -> 11.4 us
  starting transfers between devices: 0.35 us -> 9.51 us
    psum x2 -> x1, waiting for transfers between devices: 364 us -> 133 us  [run(): cubed = lax.psum(packed, 'rep')]
    convert_element_type x4 -> x1, other arithmetic: 64 us -> 4.28 us  [shards(): jnp.where(mask != 0, part + other.astype(jnp.float32), 0.0)]
    all_gather x3 -> x0, waiting for transfers between devices: 55.9 us -> none  [the longest x1 43.3 us: shards(): lax.all_gather(column_slab(current, replica, replicas, slab_rows), 'col',...]
    pallas_call x0 -> x3, Pallas kernels: none -> 47.1 us  [the longest x1 16.8 us: finish(): pl.pallas_call(functools.partial(finish_kernel, slots=slots), grid=(heigh...]
    ppermute x0 -> x5, waiting for transfers between devices: none -> 26.9 us  [the longest x1 15.6 us: gather_rows(): after = lax.ppermute(piece, 'col', down)]
    all_gather x0 -> x1, blocking collectives: none -> 21.4 us  [shards(): lax.all_gather(pattern, ('row', 'col'), axis=0)]
    convert_element_type x2 -> x0, local copies, waits for them, and re-layouts: 18.3 us -> none  [the longest x1 18.2 us: shards(): current = (hamiltonian.astype(jnp.float32) * retained).astype(jnp.bfloat16)]
    dot_general x2 -> x1, matrix products: 23 us -> 11.4 us  [shards(): part = jnp.dot(rows, current, preferred_element_type=jnp.float32)]
  transfers between devices with their start and end apart: 5 -> 6, of which waited for: 4 -> 3; matrix products, arithmetic and copies ran while one was open for 4% -> 1% of each run, Pallas kernels for 0% -> 0%
where the time goes in v1:
time: 277 us; the launch traced here: 276 us
  waiting for transfers between devices  160 us (58%)
  Pallas kernels  47.1 us (17%)
  blocking collectives  21.4 us (8%)
  between operations  17.4 us (6%)
  matrix products  11.4 us (4%)
  starting transfers between devices  9.51 us (3%)
  other arithmetic  5.27 us (2%)
  local copies, waits for them, and re-layouts  4.72 us (2%)
    psum x1, waiting for transfers between devices, run(): cubed = lax.psum(packed, 'rep')  133 us
    all_gather x1, blocking collectives, shards(): lax.all_gather(pattern, ('row', 'col'), axis=0)  21.4 us
    pallas_call x1, Pallas kernels, finish(): pl.pallas_call(functools.partial(finish_kernel, slots=slots), grid=(heigh...  16.8 us
    pallas_call x1, Pallas kernels, cube_part(): pl.pallas_call(functools.partial(cube_kernel, slots=slots), grid=(height...  16.7 us
    ppermute x1, waiting for transfers between devices, gather_rows(): after = lax.ppermute(piece, 'col', down)  15.6 us
    pallas_call x1, Pallas kernels, mask_and_pick(): pl.pallas_call(functools.partial(mask_kernel, reps=reps), grid=(height //...  13.6 us
    dot_general x1, matrix products, shards(): part = jnp.dot(rows, current, preferred_element_type=jnp.float32)  11.4 us
    ppermute x1, waiting for transfers between devices, gather_rows(): far_top = lax.ppermute(before[:cut], 'col', up)  11.3 us
  transfers between devices with their start and end apart: 6, of which 3 were waited for; matrix products, arithmetic and copies ran while one was open for 1% of the time, Pallas kernels for 0%

profile of v1, /device:TPU:1, one launch (start us, length us, event | category | flops | bytes accessed | tf_op | source)
XLA Modules:
  0.0 276.4 jit_solution(15052225004230713514)
XLA Ops:
  6.5 1.4 copy.30.pat_ref
  7.9 13.6 %mask_and_pick.1 = (bf16[3584,1792]{1,0:T(8,128)(2,1)}, bf16[112,3584]{1,0:T(8,128)(2,1)}) custom-call(s32[28,14]{1,0:T(8,128)} %copy.30.pat_ref, s32[1]{0:T(128)} %bitcast.1.rep_ref, bf16[3584,1792]{1,0:T(8,128)(2,1)} %h_ref.1), custom_call_target="tpu_custom_call" | custom-call | tf_op jit(solution)/shard_map/mask_and_pick/pallas_call | solution.py:45
  21.5 3.3 %collective-permute-start.1 = (bf16[112,3584]{1,0:T(8,128)(2,1)}, bf16[112,3584]{1,0:T(8,128)(2,1)S(1)}, u32[]{:S(2)}, u32[]{:S(2)}) collective-permute-start(bf16[112,3584]{1,0:T(8,128)(2,1)} %get-tuple-element.99), channel_id=1, source_target_pairs={{0,48},{16,0},{32,16},{48,32},{1,49},{17,1},{33,17},{49,33},{2,50}... | collective-permute-start | bytes 2408456 | tf_op jit(solution)/shard_map/ppermute | solution.py:172
  24.8 1.3 constant_dynamic-update-slice_fusion.4
  26.1 15.6 %collective-permute-done.1 = bf16[112,3584]{1,0:T(8,128)(2,1)S(1)} collective-permute-done((bf16[112,3584]{1,0:T(8,128)(2,1)}, bf16[112,3584]{1,0:T(8,128)(2,1)S(1)}, u32[]{:S(2)}, u32[]{:S(2)}) %collective-permute-start.1) | collective-permute-done | bytes 802848 | tf_op jit(solution)/shard_map/ppermute | solution.py:172
  41.7 3.4 %collective-permute-start.3 = (bf16[48,3584]{1,0:T(8,128)(2,1)S(1)}, bf16[48,3584]{1,0:T(8,128)(2,1)S(1)}, u32[]{:S(2)}, u32[]{:S(2)}) collective-permute-start(bf16[48,3584]{1,0:T(8,128)(2,1)S(1)} %slice.11), channel_id=1, source_target_pairs={{0,48},{16,0},{32,16},{48,32},{1,49},{17,1},{33,17},{49,33},{2,50}... | collective-permute-start | bytes 1032200 | tf_op jit(solution)/shard_map/ppermute | solution.py:175
  45.2 0.1 collective-permute-start.2
  45.4 11.3 %collective-permute-done.2 = bf16[64,3584]{1,0:T(8,128)(2,1)S(1)} collective-permute-done((bf16[64,3584]{1,0:T(8,128)(2,1)S(1)}, bf16[64,3584]{1,0:T(8,128)(2,1)S(1)}, u32[]{:S(2)}, u32[]{:S(2)}) %collective-permute-start.2) | collective-permute-done | bytes 458784 | tf_op jit(solution)/shard_map/ppermute | solution.py:174
  56.7 11.4 %fusion.3 = (bf16[448,1792]{1,0:T(8,128)(2,1)}, f32[448,1792]{1,0:T(8,128)}) fusion(bf16[448,3584]{1,0:T(8,128)(2,1)S(1)} %constant_dynamic-update-slice_fusion, bf16[3584,1792]{1,0:T(8,128)(2,1)} %get-tuple-element.100), kind=kOutput, calls=%fused_computation.23 | convolution fusion | flops 5755387904 | bytes 20873216 | tf_op jit(solution)/shard_map/dot_general | solution.py:202
  68.1 2.7 collective-permute-start.4
  70.9 0.1 add.120
  71.0 21.4 %all-gather.1 = s32[8,28,14]{1,2,0:T(8,128)S(1)} all-gather(s32[1,28,14]{1,2,0:T(8,128)S(1)} %bitcast.14), channel_id=2, replica_groups=mesh['row'=2,'col'=4,'rep'=16] {'row','col'}, dimensions={0}, use_global_device_ids=true | all-gather | bytes 14112 | tf_op jit(solution)/shard_map/all_gather | solution.py:187
  92.4 0.2 reduce_sum.9
  92.6 0.6 reduce_max.9
  97.2 0.1 reshape.106
  97.3 0.1 copy.32
  97.4 0.6 gather_fusion
  98.0 0.3 broadcast_in_dim.5
  98.3 4.3 %select_convert_fusion = bf16[448,1792]{1,0:T(8,128)(2,1)} fusion(f32[448,1792]{1,0:T(8,128)} %get-tuple-element.187, bf16[448,1792]{1,0:T(8,128)(2,1)} %collective-permute-done.4, pred[56,8,14,128]{3,2,1,0:T(8,128)(4,1)S(1)} %bitcast.13), kind=kLoop, calls=%fused_computation.1 | loop fusion | flops 3211264 | bytes 7225344 | tf_op jit(solution)/shard_map/convert_element_type | solution.py:204
  102.6 167.0 %conditional.1 = (bf16[3584,1792]{1,0:T(8,128)(2,1)}) conditional(s32[]{:T(128)} %clamp.3, (s32[28,14]{0,1:T(8,128)S(1)}, bf16[448,3584]{1,0:T(8,128)(2,1)S(1)}, bf16[448,1792]{1,0:T(8,128)(2,1)}, bf16[3584,1792]{1,0:T(8,128)(2,1)}) %tuple.77, (s32[28,14]{0,1:T(8,128)S(1)}, bf16[448,3584]{1,0:T(8,128)(2,1)S(1)}, ...), branch_computations={%region_2.4_spmd, %region_4.6_spmd, %region_6.8_spmd, %region_8.10... | conditional | flops 6553600 | bytes 78646384 | solution.py:214
  102.6 0.7 copy.36.pat_ref
  103.3 16.7 %cube_part.10 = bf16[224,128,128]{2,1,0:T(8,128)(2,1)} custom-call(s32[28,14]{1,0:T(8,128)} %copy.36.pat_ref, bf16[448,3584]{1,0:T(8,128)(2,1)S(1)} %get-tuple-element.83.g_ref, bf16[448,1792]{1,0:T(8,128)(2,1)} %get-tuple-element.84.q_ref), custom_call_target="tpu_custom_call" | custom-call | tf_op jit(solution)/shard_map/cond/branch_3_fun/cube_part/pallas_call | solution.py:108
  120.0 132.8 %all-reduce.14.cloned.1.call-done.cubed_ref = bf16[224,128,128]{2,1,0:T(8,128)(2,1)} async-done(((bf16[224,128,128]{2,1,0:T(8,128)(2,1)}), bf16[224,128,128]{2,1,0:T(8,128)(2,1)}) %all-reduce.14.cloned.1.call-update) | async-done | bytes 7340048 | tf_op jit(solution)/shard_map/cond/branch_3_fun/psum | solution.py:209
  252.8 16.8 %finish.10 = bf16[3584,1792]{1,0:T(8,128)(2,1)} custom-call(s32[28,14]{1,0:T(8,128)} %copy.36.pat_ref, bf16[3584,1792]{1,0:T(8,128)(2,1)} %get-tuple-element.82.h_ref, bf16[224,128,128]{2,1,0:T(8,128)(2,1)} %all-reduce.14.cloned.1.call-done.cubed_ref), custom_call_target="tpu_custom_call" | custom-call | tf_op jit(solution)/shard_map/cond/branch_3_fun/finish/pallas_call | solution.py:151
  (24 shorter events, 0.4 us)
Async XLA Ops:
  21.5 20.2 %collective-permute-start.1 = (bf16[112,3584]{1,0:T(8,128)(2,1)}, bf16[112,3584]{1,0:T(8,128)(2,1)S(1)}, u32[]{:S(2)}, u32[]{:S(2)}) collective-permute-start(bf16[112,3584]{1,0:T(8,128)(2,1)} %get-tuple-element.99), channel_id=1, source_target_pairs={{0,48},{16,0},{32,16},{48,32},{1,49},{17,1},{33,17},{49,33},{2,50}... | collective-permute-start | bytes 2408456 | tf_op jit(solution)/shard_map/ppermute | solution.py:172
  24.8 20.3 %collective-permute-start = (bf16[112,3584]{1,0:T(8,128)(2,1)}, bf16[112,3584]{1,0:T(8,128)(2,1)S(1)}, u32[]{:S(2)}, u32[]{:S(2)}) collective-permute-start(bf16[112,3584]{1,0:T(8,128)(2,1)} %get-tuple-element.99), channel_id=1, source_target_pairs={{0,16},{16,32},{32,48},{48,0},{1,17},{17,33},{33,49},{49,1},{2,18}... | collective-permute-start | bytes 2408456 | tf_op jit(solution)/shard_map/ppermute | solution.py:171
  41.7 14.9 %collective-permute-start.3 = (bf16[48,3584]{1,0:T(8,128)(2,1)S(1)}, bf16[48,3584]{1,0:T(8,128)(2,1)S(1)}, u32[]{:S(2)}, u32[]{:S(2)}) collective-permute-start(bf16[48,3584]{1,0:T(8,128)(2,1)S(1)} %slice.11), channel_id=1, source_target_pairs={{0,48},{16,0},{32,16},{48,32},{1,49},{17,1},{33,17},{49,33},{2,50}... | collective-permute-start | bytes 1032200 | tf_op jit(solution)/shard_map/ppermute | solution.py:175
  45.2 11.5 %collective-permute-start.2 = (bf16[64,3584]{1,0:T(8,128)(2,1)S(1)}, bf16[64,3584]{1,0:T(8,128)(2,1)S(1)}, u32[]{:S(2)}, u32[]{:S(2)}) collective-permute-start(bf16[64,3584]{1,0:T(8,128)(2,1)S(1)} %slice.10), channel_id=1, source_target_pairs={{0,16},{16,32},{32,48},{48,0},{1,17},{17,33},{33,49},{49,1},{2,18}... | collective-permute-start | bytes 1376264 | tf_op jit(solution)/shard_map/ppermute | solution.py:174
  56.7 14.1 %copy-start.1 = (s32[4]{0:T(128)S(1)}, s32[4]{0:T(128)}, u32[]{:S(2)}) copy-start(s32[4]{0:T(128)} %constant.74.clone) | copy-start | bytes 52
  56.7 14.3 %copy-start = (s32[28,14]{0,1:T(8,128)S(1)}, s32[28,14]{0,1:T(8,128)}, u32[]{:S(2)}) copy-start(s32[28,14]{0,1:T(8,128)} %param.11) | copy-start | bytes 4708
  68.1 29.9 %collective-permute-start.4 = (bf16[448,1792]{1,0:T(8,128)(2,1)}, bf16[448,1792]{1,0:T(8,128)(2,1)}, u32[]{:S(2)}, u32[]{:S(2)}) collective-permute-start(bf16[448,1792]{1,0:T(8,128)(2,1)} %get-tuple-element.186), channel_id=1, source_target_pairs={{0,64},{64,0},{1,65},{65,1},{2,66},{66,2},{3,67},{67,3},{4,68},{68... | collective-permute-start | bytes 4816904 | tf_op jit(solution)/shard_map/ppermute | solution.py:203
  102.6 150.2 %all-reduce.14.cloned.1.call-start = ((), (), s32[]{:S(2)}) async-start(), calls=%async_computation.3 | async-start | bytes 14680064 | tf_op jit(solution)/shard_map/cond/branch_3_fun/psum | solution.py:209
Sparse Core Ops, SparseCore 0:
  120.1 132.6 all-reduce.13
